TPU v7x, 32 devices: a whole 2x2x4 slice. The times are simulated.
32 devices in a mesh: grp: 4 (over y, x), dom: 8 (over z, core).
Axes of the slice: x: 2, y: 2, z: 4, core: 2. Of those that a mesh axis runs over, the one named last changes fastest.
Arguments:
- features: bfloat16 [98304, 256], P(('grp', 'dom')), may hold values from -6 to 6
- boundary_cache: float32 [8192, 256], P(('grp', 'dom')), may hold values from -6 to 6
- adjacency: bfloat16 [768, 2, 128, 128], P(('grp', 'dom')), may hold values from -0.375 to 0.375
- neighbor: int32 [768, 2], P(('grp', 'dom')), may hold values from 0 to 31
- counts: int32 [768], P(('grp', 'dom')), may hold values from 1 to 2
- wanted: int32 [32, 8], P(('grp', 'dom')), may hold values from 0 to 1
- weight_in: bfloat16 [512, 512], replicated, may hold values from -0.25 to 0.25
- weight_out: bfloat16 [512, 256], replicated, may hold values from -0.25 to 0.25
- cotangent: bfloat16 [98304, 256], P(('grp', 'dom')), may hold values from -6 to 6
Outputs:
- grad_features: bfloat16 [98304, 256], P(('grp', 'dom'))
- grad_weight_in: float32 [512, 512], P('dom')
- grad_weight_out: float32 [512, 256], P('dom')
Inputs may be any that keep to these rules, and one draw needn't show every extreme that they name: `neighbor`: A value under 24 names a block of the same partition; a value 24 + q names the boundary block that the partition reads from partition q of its group. Slots from counts[b] on are padding and carry no edges.
All inputs are finite; a program needn't handle non-finite values.
Results may differ from a plain program's by a relative error of at most 0.0054.
Values may be sent and summed in bfloat16 or wider, within the bound.
A program may use at most 128 MiB of HBM per device.

v0:
```python
import functools
import math

import jax
import jax.numpy as jnp
import numpy as np
from jax import lax
from jax.experimental import pallas as pl
from jax.experimental.pallas import tpu as pltpu
from jax.sharding import PartitionSpec as P

F32, BF16 = jnp.float32, jnp.bfloat16
TILE = 512
NT_DIMS = (((1,), (1,)), ((), ()))


def mm(a, b):
    return jnp.dot(a, b, preferred_element_type=F32)


def mm_nt(a, b):
    return lax.dot_general(a, b, NT_DIMS, preferred_element_type=F32)


def layer_kernel(
    n_grp, n_dom,
    nbr, cnt, prev, last_of, wnt, feat_h, cache_h, adj_h, win_h, wout_h, cot_h,
    out_h, gw_in_h, gw_out_h,
    src, cache, adj, win, wout, cot, win_t, pre2, gh, gps, acc_in, acc_out,
    base, terms, out, own1, sb1, rb1, chip, sb2, rb2, sb3, rb3, gat4,
    load_sem, out_sem, b_send, b_recv, s1, r1, s2, r2, s3, r3, s4, r4,
):
    nb, slots, blk, _ = adj.shape
    exports = cache.shape[0] // blk
    line = n_dom // 2
    tiles = cot.shape[0]
    per = TILE // blk
    ch = cot.shape[2]
    hid_n = wout.shape[0]
    rows = rb1.shape[1]
    none = nb + n_dom * exports

    g = lax.axis_index("grp")
    d = lax.axis_index("dom")
    z, c = d // 2, lax.rem(d, 2)
    pair = z * 2 + (1 - c)

    def load(i, a, b):
        return pltpu.make_async_copy(a, b, load_sem.at[i])

    loads = [
        load(0, cache_h, cache),
        load(1, wout_h, wout),
        load(2, cot_h, cot),
        load(3, win_h, win),
        load(4, feat_h, src.at[pl.ds(0, nb)]),
        load(5, adj_h, adj),
    ]
    for item in loads:
        item.start()

    barrier = pltpu.get_barrier_semaphore()
    peers = [(g, pair)]
    peers += [(g, 2 * lax.rem(z + k, line) + c) for k in range(1, line)]
    peers += [(lax.rem(g + k, n_grp), d) for k in range(1, n_grp)]
    for peer in peers:
        pl.semaphore_signal(barrier, inc=1, device_id=peer, device_id_type=pl.DeviceIdType.MESH)

    loads[0].wait()
    src[pl.ds(nb + d * exports, exports)] = cache[...].astype(BF16).reshape(exports, blk, ch)
    pl.semaphore_wait(barrier, len(peers))

    def remote(a, b, send, recv, where):
        return pltpu.make_async_remote_copy(
            src_ref=a, dst_ref=b, send_sem=send, recv_sem=recv,
            device_id=where, device_id_type=pl.DeviceIdType.MESH,
        )

    def spread(q, e, way):
        part = src.at[nb + q * exports + e]
        to = (d + 2, d - 2, pair)[way]
        return remote(part, part, b_send.at[q, e, way], b_recv.at[q, e], (g, to))

    not_last, not_first = z < line - 1, z > 0
    for e in range(exports):
        pl.when(not_last)(lambda: spread(d, e, 0).start())
        pl.when(not_first)(lambda: spread(d, e, 1).start())
    for e in range(exports):
        spread(d, e, 2).start()

    for item in loads[1:5]:
        item.wait()
    win_t[...] = win[...].astype(F32).T.astype(BF16)
    src[pl.ds(none, exports)] = jnp.zeros((exports, blk, ch), BF16)
    terms[0] = jnp.zeros((ch, blk), F32)

    def early(i, carry):
        gh[i] = mm_nt(wout[...], cot[i])
        own = src[pl.ds(i * per, per)].reshape(TILE, ch)
        pre2[i] = mm_nt(win_t[:, ch:], own)
        return carry

    done = 0
    for k in range(1, line):
        upto = tiles * k // (line - 1)
        lax.fori_loop(done, upto, early, 0)
        done = upto

        @pl.when(z - k >= 0)
        def _():
            for e in range(exports):
                spread(d - 2 * k, e, 0).wait_recv()
                pl.when(not_last)(lambda: spread(d - 2 * k, e, 0).start())
                spread(d - 2 * k, e, 2).start()

        @pl.when(z + k < line)
        def _():
            for e in range(exports):
                spread(d + 2 * k, e, 1).wait_recv()
                pl.when(not_first)(lambda: spread(d + 2 * k, e, 1).start())
                spread(d + 2 * k, e, 2).start()

    acc_in[...] = jnp.zeros_like(acc_in)
    acc_out[...] = jnp.zeros_like(acc_out)
    loads[5].wait()
    for zz in range(line):
        for e in range(exports):
            spread(2 * zz + 1 - c, e, 2).wait_recv()

    def source(b, s):
        n = jnp.where(s < cnt[b], nbr[s, b], nb + n_dom)
        far = jnp.maximum(n - nb, 0)
        pick = wnt[0, jnp.minimum(far, n_dom - 1)]
        return src[jnp.where(n < nb, n, nb + far * exports + pick)]

    def main(i, carry):
        parts = []
        for k in range(per):
            b = i * per + k
            left = jnp.concatenate([adj[b, s] for s in range(slots)], axis=1)
            right = jnp.concatenate([source(b, s) for s in range(slots)], axis=0)
            parts.append(mm(left, right).astype(BF16))
        agg = jnp.concatenate(parts, axis=0)
        pre = pre2[i] + mm_nt(win_t[:, :ch], agg)
        sg = 0.5 + 0.5 * jnp.tanh(0.5 * pre)
        h = pre * sg
        gp = (gh[i] * (sg + h * (1.0 - sg))).astype(BF16)
        gps[i] = gp
        own = src[pl.ds(i * per, per)].reshape(TILE, ch)
        for m, part in enumerate((agg, own)):
            term = mm(gp, part)
            for j in range(ch // (2 * rows)):
                at = m * (ch // (2 * rows)) + j
                acc_in[at] += term[:, j * 2 * rows : (j + 1) * 2 * rows]
        acc_out[...] += mm(h.astype(BF16), cot[i]).reshape(acc_out.shape)
        return carry

    lax.fori_loop(0, tiles, main, 0)

    def late(i, carry):
        gj = mm(win[...], gps[i])
        gagg = gj[:ch].astype(BF16)
        for k in range(per):
            b = i * per + k
            cols = slice(k * blk, (k + 1) * blk)
            base[b] = gj[ch:, cols]
            both = mm(gagg[:, cols], jnp.concatenate([adj[b, s] for s in range(slots)], axis=1))
            for s in range(slots):
                terms[1 + b * slots + s] = both[:, s * blk : (s + 1) * blk]
        return carry

    def chain(b, carry):
        for s in range(slots):
            terms[1 + b * slots + s] += terms[prev[s, b]]
        return carry

    def write(b, carry):
        out[b] = (base[b] + terms[last_of[b]]).T.astype(BF16)
        return carry

    order = [lax.rem(z + k, line) for k in range(1, line + 1)]

    def step1(zz):
        return remote(sb1.at[zz, 1 - c], rb1.at[zz], s1.at[zz], r1.at[zz], (g, pair))

    for zz in order:
        whole = jnp.concatenate([acc_in[zz].T, acc_out[zz]], axis=1)
        whole = whole.reshape(2, rows, whole.shape[1])
        own1[zz] = whole
        sb1[zz] = whole.astype(BF16)
        step1(zz).start()

    def step2(zz, k):
        to = lax.rem(g + k, n_grp)
        return remote(
            sb2.at[zz, to], rb2.at[k - 1, zz], s2.at[k - 1, zz], r2.at[k - 1, zz], (to, d)
        )

    for zz in order:
        step1(zz).wait_recv()
        both = (own1[zz, c] + rb1[zz].astype(F32)).reshape(chip.shape[1:])
        chip[zz] = both
        sb2[zz] = both.astype(BF16)
        for k in range(1, n_grp):
            step2(zz, k).start()

    lax.fori_loop(0, tiles, late, 0)
    def step3(k):
        to = lax.rem(z + k, line)
        return remote(sb3.at[k - 1], rb3.at[k - 1], s3.at[k - 1], r3.at[k - 1], (g, 2 * to + c))

    total = None
    for k, zz in enumerate(order, 1):
        total = chip[zz, g]
        for j in range(1, n_grp):
            step2(zz, j).wait_recv()
            total += rb2[j - 1, zz].astype(F32)
        if k < line:
            sb3[k - 1] = total.astype(BF16)
            step3(k).start()
    lax.fori_loop(0, nb, chain, 0)
    for k in range(1, line):
        step3(k).wait_recv()
        total += rb3[k - 1].astype(F32)

    def step4(k):
        to = lax.rem(g + k, n_grp)
        return remote(gat4.at[g], gat4.at[g], s4.at[k - 1], r4.at[k - 1], (to, d))

    def arrive4(k):
        there = gat4.at[lax.rem(g - k + n_grp, n_grp)]
        return remote(there, there, s4.at[k - 1], r4.at[k - 1], (lax.rem(g + k, n_grp), d))

    gat4[g] = total.astype(BF16)
    for k in range(1, n_grp):
        step4(k).start()
    lax.fori_loop(0, nb, write, 0)
    store = pltpu.make_async_copy(out, out_h, out_sem.at[0])
    store.start()
    for k in range(1, n_grp):
        arrive4(k).wait_recv()
    last = [
        pltpu.make_async_copy(gat4.at[:, :, pl.ds(0, hid_n)], gw_in_h, out_sem.at[1]),
        pltpu.make_async_copy(gat4.at[:, :, pl.ds(hid_n, ch)], gw_out_h, out_sem.at[2]),
    ]
    for item in last:
        item.start()

    for e in range(exports):
        pl.when(not_last)(lambda: spread(d, e, 0).wait_send())
        pl.when(not_first)(lambda: spread(d, e, 1).wait_send())
        spread(d, e, 2).wait_send()
    for k in range(1, line):

        @pl.when(z - k >= 0)
        def _():
            for e in range(exports):
                pl.when(not_last)(lambda: spread(d - 2 * k, e, 0).wait_send())
                spread(d - 2 * k, e, 2).wait_send()

        @pl.when(z + k < line)
        def _():
            for e in range(exports):
                pl.when(not_first)(lambda: spread(d + 2 * k, e, 1).wait_send())
                spread(d + 2 * k, e, 2).wait_send()

    for zz in order:
        step1(zz).wait_send()
        for k in range(1, n_grp):
            step2(zz, k).wait_send()
    for k in range(1, line):
        step3(k).wait_send()
    for k in range(1, n_grp):
        step4(k).wait_send()
    store.wait()
    for item in last:
        item.wait()


def chains(targets, counts, nb):
    slots = targets.shape[0]
    live = jnp.arange(slots)[:, None] < counts[None, :]
    key = jnp.where(live, targets, -1)
    place = 1 + np.arange(nb)[None, :] * slots + np.arange(slots)[:, None]
    place = jnp.asarray(place.astype(np.int32))
    same = key[:, :, None, None] == key[None, None]
    same &= place[None, None] < place[:, :, None, None]
    prev = jnp.max(jnp.where(same, place[None, None], 0), axis=(2, 3))
    mine = key[None] == jnp.arange(nb)[:, None, None]
    return prev, jnp.max(jnp.where(mine, place[None], 0), axis=(1, 2))


def fast_local(
    features, boundary_cache, adjacency, neighbor, counts, wanted, weight_in, weight_out, cotangent
):
    nb, slots, blk, _ = adjacency.shape
    node_rows, ch = features.shape
    hid_n = weight_out.shape[0]
    n_grp, n_dom = lax.axis_size("grp"), lax.axis_size("dom")
    line = n_dom // 2
    tiles = node_rows // TILE
    exports = boundary_cache.shape[0] // blk
    rows = hid_n // n_dom
    wide = hid_n + ch
    share = rows // n_grp
    any_spec = pl.BlockSpec(memory_space=pl.ANY)
    smem = pl.BlockSpec(memory_space=pltpu.SMEM)
    dma = pltpu.SemaphoreType.DMA
    V = pltpu.VMEM
    nodes = node_rows
    cost = pl.CostEstimate(
        flops=2 * nodes * hid_n * (7 * ch), bytes_accessed=8 * nodes * ch,
        transcendentals=nodes * hid_n,
    )
    targets = neighbor.T
    prev, last_of = chains(targets, counts, nb)
    out, gw_in, gw_out = pl.pallas_call(
        functools.partial(layer_kernel, n_grp, n_dom),
        out_shape=(
            jax.ShapeDtypeStruct((nb, blk, ch), BF16),
            jax.ShapeDtypeStruct((n_grp, share, hid_n), BF16),
            jax.ShapeDtypeStruct((n_grp, share, ch), BF16),
        ),
        in_specs=[smem] * 5 + [any_spec] * 6,
        out_specs=(any_spec,) * 3,
        scratch_shapes=[
            V((nb + (n_dom + 1) * exports, blk, ch), BF16),
            V(boundary_cache.shape, F32),
            V(adjacency.shape, BF16),
            V(weight_in.shape, BF16),
            V(weight_out.shape, BF16),
            V((tiles, TILE, ch), BF16),
            V((hid_n, 2 * ch), BF16),
            V((tiles, hid_n, TILE), F32),
            V((tiles, hid_n, TILE), F32),
            V((tiles, hid_n, TILE), BF16),
            V((line, hid_n, 2 * rows), F32),
            V((line, 2 * rows, ch), F32),
            V((nb, ch, blk), F32),
            V((nb * slots + 1, ch, blk), F32),
            V((nb, blk, ch), BF16),
            V((line, 2, rows, wide), F32),
            V((line, 2, rows, wide), BF16),
            V((line, rows, wide), BF16),
            V((line, n_grp, share, wide), F32),
            V((line, n_grp, share, wide), BF16),
            V((n_grp - 1, line, share, wide), BF16),
            V((line - 1, share, wide), BF16),
            V((line - 1, share, wide), BF16),
            V((n_grp, share, wide), BF16),
            dma((6,)), dma((3,)),
            dma((n_dom, exports, 3)), dma((n_dom, exports)),
            dma((line,)), dma((line,)),
            dma((n_grp - 1, line)), dma((n_grp - 1, line)),
            dma((line - 1,)), dma((line - 1,)),
            dma((n_grp - 1,)), dma((n_grp - 1,)),
        ],
        compiler_params=pltpu.CompilerParams(
            collective_id=0, has_side_effects=True, vmem_limit_bytes=56 * 2**20
        ),
        cost_estimate=cost,
    )(
        targets, counts, prev, last_of, wanted, features.reshape(nb, blk, ch), boundary_cache, adjacency,
        weight_in, weight_out, cotangent.reshape(tiles, TILE, ch),
    )
    scale = 1.0 / math.sqrt(node_rows * n_grp * n_dom)
    gw_in, gw_out = (x.reshape(rows, -1).astype(F32) * scale for x in (gw_in, gw_out))
    return out.reshape(node_rows, ch), gw_in, gw_out


def local(
    features, boundary_cache, adjacency, neighbor, counts, wanted, weight_in, weight_out, cotangent
):
    nblocks = adjacency.shape[0]
    slot_total = adjacency.shape[1]
    block_rows = adjacency.shape[2]
    channels = features.shape[1]
    node_rows = nblocks * block_rows
    partners = lax.axis_size("dom")
    cache_copy = boundary_cache.astype(jnp.bfloat16)
    exported = cache_copy.reshape(-1, block_rows, channels)
    export_total = exported.shape[0]
    exported_all = lax.all_gather(cache_copy, "dom", axis=0, tiled=True).reshape(
        partners, export_total, block_rows, channels
    )
    selected = wanted[0]
    boundary = exported_all[:, 0]
    boundary = jnp.where((selected == 1)[:, None, None], exported_all[:, 1], boundary)
    owned = features.reshape(nblocks, block_rows, channels)
    sources = jnp.concatenate([owned, boundary], 0)
    active = jnp.arange(slot_total)[None, :] < counts[:, None]
    chosen = sources[neighbor]
    chosen = jnp.where(active[:, :, None, None], chosen, jnp.zeros_like(chosen))
    aggregate = jnp.einsum("bsij,bsjf->bif", adjacency, chosen, preferred_element_type=jnp.float32)
    aggregate = aggregate.astype(jnp.bfloat16).reshape(node_rows, channels)
    joined = jnp.concatenate([aggregate, features], 1)
    preact = jnp.dot(joined, weight_in, preferred_element_type=jnp.float32)
    gating = jax.nn.sigmoid(preact)
    hidden = (preact * gating).astype(jnp.bfloat16)
    grad_hidden = jnp.einsum("nf,hf->nh", cotangent, weight_out, preferred_element_type=jnp.float32)
    grad_preact = (grad_hidden * gating * (1.0 + preact * (1.0 - gating))).astype(jnp.bfloat16)
    grad_joined = jnp.einsum(
        "nh,ch->nc", grad_preact, weight_in, preferred_element_type=jnp.float32
    )
    grad_aggregate = (
        grad_joined[:, :channels].astype(jnp.bfloat16).reshape(nblocks, block_rows, channels)
    )
    backward = jnp.einsum(
        "bsji,bjf->bsif", adjacency, grad_aggregate, preferred_element_type=jnp.float32
    )
    local_hit = active & (neighbor < nblocks)
    routing = (neighbor[None, :, :] == jnp.arange(nblocks)[:, None, None]) & local_hit[None]
    spread = jnp.einsum(
        "cbs,bsif->cif", routing.astype(jnp.float32), backward, precision=lax.Precision.HIGHEST
    )
    grad_features = (grad_joined[:, channels:] + spread.reshape(node_rows, channels)).astype(
        jnp.bfloat16
    )
    node_total = node_rows * lax.axis_size("grp") * partners
    loss_scale = 1.0 / math.sqrt(node_total)
    rows_in = weight_in.shape[0] // partners
    rows_out = weight_out.shape[0] // partners
    summed = lax.psum(
        (
            jnp.einsum("nc,nh->ch", joined, grad_preact, preferred_element_type=jnp.float32)
            * loss_scale,
            jnp.einsum("nh,nf->hf", hidden, cotangent, preferred_element_type=jnp.float32)
            * loss_scale,
        ),
        ("grp", "dom"),
    )
    position = lax.axis_index("dom")
    grad_weight_in = lax.dynamic_slice_in_dim(summed[0], position * rows_in, rows_in, 0)
    grad_weight_out = lax.dynamic_slice_in_dim(summed[1], position * rows_out, rows_out, 0)
    return (grad_features, grad_weight_in, grad_weight_out)


def solution(mesh):
    in_specs = (
        P(("grp", "dom"), None),
        P(("grp", "dom"), None),
        P(("grp", "dom"), None, None, None),
        P(("grp", "dom"), None),
        P(("grp", "dom")),
        P(("grp", "dom"), None),
        P(),
        P(),
        P(("grp", "dom"), None),
    )
    out_specs = (P(("grp", "dom"), None), P("dom", None), P("dom", None))
    n_grp, n_dom = mesh.shape["grp"], mesh.shape["dom"]

    def program(*args):
        rows = args[7].shape[0] // n_dom
        nodes = args[0].shape[0] // (n_grp * n_dom)
        fits = rows % (16 * n_grp) == 0 and (2 * rows) % 128 == 0 and nodes % TILE == 0
        body = fast_local if fits else local
        return sharded(body)(*args)

    def sharded(body):
        return jax.shard_map(
            body, mesh=mesh, in_specs=in_specs, out_specs=out_specs, check_vma=False
        )

    return program
```

profile of v0, /device:TPU:0, one launch (start us, length us, event | category | flops | bytes accessed | tf_op | source)
XLA Modules:
  0.0 48.9 jit_solution(14754670112862052072)
XLA Ops:
  0.6 0.7 %compare_select_fusion = s32[2,24]{1,0:T(2,128)S(1)} fusion(s32[24]{0:T(128)} %cnt.1, s32[24,2]{0,1:T(2,128)} %param.13), kind=kLoop, calls=%fused_computation.5 | loop fusion | flops 96 | bytes 480 | tf_op jit(solution)/shard_map/jit(_where)/select_n | solution.py:283
  1.3 1.3 %select_reduce_fusion.1.last_of = s32[24]{0:T(128)} fusion(s32[2,24]{1,0:T(2,128)} %constant.4.clone, s32[2,24]{1,0:T(2,128)S(1)} %compare_select_fusion), kind=kLoop, calls=%fused_computation.3 | loop fusion | flops 3432 | bytes 480 | tf_op jit(solution)/shard_map/reduce_max | solution.py:290
  2.6 1.5 %select_reduce_fusion.prev = s32[2,24]{1,0:T(2,128)} fusion(s32[2,24]{1,0:T(2,128)} %constant.4.clone, s32[2,24]{1,0:T(2,128)S(1)} %compare_select_fusion), kind=kLoop, calls=%fused_computation.2 | loop fusion | flops 11472 | bytes 576 | tf_op jit(solution)/shard_map/reduce_max | solution.py:288
  4.1 39.2 %shard_map.121 = (bf16[24,128,256]{2,1,0:T(8,128)(2,1)}, bf16[4,16,512]{2,1,0:T(8,128)(2,1)}, bf16[4,16,256]{2,1,0:T(8,128)(2,1)}) custom-call(s32[2,24]{1,0:T(2,128)} %bitcast.10, s32[24]{0:T(128)} %cnt.1, s32[2,24]{1,0:T(2,128)} %select_reduce_fusion.prev, s32[24]{0:T(128)} %select_reduce_fusion.1.last_of, s32[1,8]{1,0:T(1,128)} %wnt.1, ...), custom_call_target="tpu_custom_call" | custom-call | flops 5637144576 | bytes 6291456 | tf_op jit(solution)/shard_map/pallas_call | solution.py:317
  43.4 1.4 %convert_multiply_fusion.1 = f32[4,16,256]{2,1,0:T(8,128)} fusion(bf16[4,16,256]{2,1,0:T(8,128)(2,1)} %get-tuple-element.8), kind=kLoop, calls=%fused_computation.1 | loop fusion | flops 32768 | bytes 98304 | tf_op jit(solution)/shard_map/mul | solution.py:367
  44.8 1.5 %convert_multiply_fusion = f32[4,16,512]{2,1,0:T(8,128)} fusion(bf16[4,16,512]{2,1,0:T(8,128)(2,1)} %get-tuple-element.7), kind=kLoop, calls=%fused_computation | loop fusion | flops 65536 | bytes 196608 | tf_op jit(solution)/shard_map/mul | solution.py:367
  46.3 2.7 %copy.14 = bf16[3072,256]{1,0:T(8,128)(2,1)} copy(bf16[3072,256]{1,0:T(8,128)(2,1)} %bitcast.7) | data formatting | bytes 3145728
where the time goes:
time: 49.2 us; the launch traced here: 48.9 us
  Pallas kernels  39.2 us (80%)
  other arithmetic  6.42 us (13%)
  local copies, waits for them, and re-layouts  2.65 us (5%)
  between operations  0.64 us (1%)
    pallas_call x1, Pallas kernels, fast_local(): pl.pallas_call(functools.partial(layer_kernel, n_grp, n_dom), out_shape=(...  39.2 us
    mul x2, other arithmetic, fast_local(): x.reshape(rows, -1).astype(F32) * scale  2.9 us
    unnamed x1, local copies, waits for them, and re-layouts  2.65 us
    reduce_max x1, other arithmetic, chains(): prev = jnp.max(jnp.where(same, place[None, None], 0), axis=(2, 3))  1.5 us
    reduce_max x1, other arithmetic, chains(): return (prev, jnp.max(jnp.where(mine, place[None], 0), axis=(1, 2)))  1.31 us

commit v1 on v0

--- a/solution.py
+++ b/solution.py
@@ -3,7 +3,6 @@
 
 import jax
 import jax.numpy as jnp
-import numpy as np
 from jax import lax
 from jax.experimental import pallas as pl
 from jax.experimental.pallas import tpu as pltpu
@@ -24,10 +23,10 @@
 
 def layer_kernel(
     n_grp, n_dom,
-    nbr, cnt, prev, last_of, wnt, feat_h, cache_h, adj_h, win_h, wout_h, cot_h,
-    out_h, gw_in_h, gw_out_h,
-    src, cache, adj, win, wout, cot, win_t, pre2, gh, gps, acc_in, acc_out,
-    base, terms, out, own1, sb1, rb1, chip, sb2, rb2, sb3, rb3, gat4,
+    nbr, cnt, wnt, feat_h, cache_h, adj_h, win_h, wout_h, cot_h,
+    out_h, gw_h,
+    src, cache, adj, win, wout, cot, win_t, pre2, gh, gps, hids, aggs, acc_in, acc_out,
+    base, terms, out, own1, sb1, rb1, chip, sb2, rb2, sb3, rb3, gat4, table, links,
     load_sem, out_sem, b_send, b_recv, s1, r1, s2, r2, s3, r3, s4, r4,
 ):
     nb, slots, blk, _ = adj.shape
@@ -88,6 +87,30 @@
     for e in range(exports):
         spread(d, e, 2).start()
 
+    pairs = nb * slots
+    lane = lax.broadcasted_iota(jnp.int32, table.shape, 1)
+
+    def target(b, s):
+        return jnp.where(s < cnt[b], nbr[s, b], nb + n_dom)
+
+    def ask(b, asked):
+        for s in range(slots):
+            asked = jnp.where(lane == b * slots + s, target(b, s), asked)
+        return asked
+
+    def find(b, found):
+        for s in range(slots):
+            p = b * slots + s
+            hit = jnp.logical_and(asked == target(b, s), limit > p)
+            found = jnp.where(hit, p + 1, found)
+        return found
+
+    limit = jnp.minimum(lane, pairs)
+    asked = lax.fori_loop(0, nb, ask, lane - pairs)
+    table[...] = lax.fori_loop(0, nb, find, jnp.zeros_like(lane))
+    to_links = load(6, table, links)
+    to_links.start()
+
     for item in loads[1:5]:
         item.wait()
     win_t[...] = win[...].astype(F32).T.astype(BF16)
@@ -123,17 +146,18 @@
     acc_in[...] = jnp.zeros_like(acc_in)
     acc_out[...] = jnp.zeros_like(acc_out)
     loads[5].wait()
+    to_links.wait()
     for zz in range(line):
         for e in range(exports):
             spread(2 * zz + 1 - c, e, 2).wait_recv()
 
     def source(b, s):
-        n = jnp.where(s < cnt[b], nbr[s, b], nb + n_dom)
+        n = target(b, s)
         far = jnp.maximum(n - nb, 0)
         pick = wnt[0, jnp.minimum(far, n_dom - 1)]
         return src[jnp.where(n < nb, n, nb + far * exports + pick)]
 
-    def main(i, carry):
+    def front(i):
         parts = []
         for k in range(per):
             b = i * per + k
@@ -144,18 +168,28 @@
         pre = pre2[i] + mm_nt(win_t[:, :ch], agg)
         sg = 0.5 + 0.5 * jnp.tanh(0.5 * pre)
         h = pre * sg
-        gp = (gh[i] * (sg + h * (1.0 - sg))).astype(BF16)
-        gps[i] = gp
+        gps[i] = (gh[i] * (sg + h * (1.0 - sg))).astype(BF16)
+        hids[i] = h.astype(BF16)
+        aggs[i] = agg
+
+    def weight_grads(i):
+        gp = gps[i]
         own = src[pl.ds(i * per, per)].reshape(TILE, ch)
-        for m, part in enumerate((agg, own)):
+        for m, part in enumerate((aggs[i], own)):
             term = mm(gp, part)
             for j in range(ch // (2 * rows)):
                 at = m * (ch // (2 * rows)) + j
                 acc_in[at] += term[:, j * 2 * rows : (j + 1) * 2 * rows]
-        acc_out[...] += mm(h.astype(BF16), cot[i]).reshape(acc_out.shape)
+        acc_out[...] += mm(hids[i], cot[i]).reshape(acc_out.shape)
+
+    def main(i, carry):
+        weight_grads(i - 1)
+        front(i)
         return carry
 
-    lax.fori_loop(0, tiles, main, 0)
+    front(0)
+    lax.fori_loop(1, tiles, main, 0)
+    weight_grads(tiles - 1)
 
     def late(i, carry):
         gj = mm(win[...], gps[i])
@@ -171,11 +205,11 @@
 
     def chain(b, carry):
         for s in range(slots):
-            terms[1 + b * slots + s] += terms[prev[s, b]]
+            terms[1 + b * slots + s] += terms[links[0, b * slots + s]]
         return carry
 
     def write(b, carry):
-        out[b] = (base[b] + terms[last_of[b]]).T.astype(BF16)
+        out[b] = (base[b] + terms[links[0, pairs + b]]).T.astype(BF16)
         return carry
 
     order = [lax.rem(z + k, line) for k in range(1, line + 1)]
@@ -239,12 +273,8 @@
     store.start()
     for k in range(1, n_grp):
         arrive4(k).wait_recv()
-    last = [
-        pltpu.make_async_copy(gat4.at[:, :, pl.ds(0, hid_n)], gw_in_h, out_sem.at[1]),
-        pltpu.make_async_copy(gat4.at[:, :, pl.ds(hid_n, ch)], gw_out_h, out_sem.at[2]),
-    ]
-    for item in last:
-        item.start()
+    last = pltpu.make_async_copy(gat4, gw_h, out_sem.at[1])
+    last.start()
 
     for e in range(exports):
         pl.when(not_last)(lambda: spread(d, e, 0).wait_send())
@@ -273,21 +303,23 @@
     for k in range(1, n_grp):
         step4(k).wait_send()
     store.wait()
-    for item in last:
+    last.wait()
+
+
+def finish_kernel(scale, out_a, in_a, out_b, gw_in, gw_out, sems):
+    count = sems.shape[0]
+    step = out_a.shape[0] // count
+    copies = []
+    for i in range(count):
+        part = pl.ds(i * step, step)
+        copies.append(pltpu.make_async_copy(out_a.at[part], out_b.at[part], sems.at[i]))
+    for item in copies:
+        item.start()
+    value = in_a[...].astype(F32) * scale
+    gw_in[...] = value[:, : gw_in.shape[1]]
+    gw_out[...] = value[:, gw_in.shape[1] :]
+    for item in copies:
         item.wait()
-
-
-def chains(targets, counts, nb):
-    slots = targets.shape[0]
-    live = jnp.arange(slots)[:, None] < counts[None, :]
-    key = jnp.where(live, targets, -1)
-    place = 1 + np.arange(nb)[None, :] * slots + np.arange(slots)[:, None]
-    place = jnp.asarray(place.astype(np.int32))
-    same = key[:, :, None, None] == key[None, None]
-    same &= place[None, None] < place[:, :, None, None]
-    prev = jnp.max(jnp.where(same, place[None, None], 0), axis=(2, 3))
-    mine = key[None] == jnp.arange(nb)[:, None, None]
-    return prev, jnp.max(jnp.where(mine, place[None], 0), axis=(1, 2))
 
 
 def fast_local(
@@ -303,7 +335,9 @@
     rows = hid_n // n_dom
     wide = hid_n + ch
     share = rows // n_grp
+    links_wide = -(-(nb * slots + nb) // 128) * 128
     any_spec = pl.BlockSpec(memory_space=pl.ANY)
+    vmem = pl.BlockSpec(memory_space=pltpu.VMEM)
     smem = pl.BlockSpec(memory_space=pltpu.SMEM)
     dma = pltpu.SemaphoreType.DMA
     V = pltpu.VMEM
@@ -312,17 +346,14 @@
         flops=2 * nodes * hid_n * (7 * ch), bytes_accessed=8 * nodes * ch,
         transcendentals=nodes * hid_n,
     )
-    targets = neighbor.T
-    prev, last_of = chains(targets, counts, nb)
-    out, gw_in, gw_out = pl.pallas_call(
+    out, gw = pl.pallas_call(
         functools.partial(layer_kernel, n_grp, n_dom),
         out_shape=(
             jax.ShapeDtypeStruct((nb, blk, ch), BF16),
-            jax.ShapeDtypeStruct((n_grp, share, hid_n), BF16),
-            jax.ShapeDtypeStruct((n_grp, share, ch), BF16),
+            jax.ShapeDtypeStruct((n_grp, share, wide), BF16),
         ),
-        in_specs=[smem] * 5 + [any_spec] * 6,
-        out_specs=(any_spec,) * 3,
+        in_specs=[smem] * 3 + [any_spec] * 6,
+        out_specs=(any_spec,) * 2,
         scratch_shapes=[
             V((nb + (n_dom + 1) * exports, blk, ch), BF16),
             V(boundary_cache.shape, F32),
@@ -334,6 +365,8 @@
             V((tiles, hid_n, TILE), F32),
             V((tiles, hid_n, TILE), F32),
             V((tiles, hid_n, TILE), BF16),
+            V((tiles, hid_n, TILE), BF16),
+            V((tiles, TILE, ch), BF16),
             V((line, hid_n, 2 * rows), F32),
             V((line, 2 * rows, ch), F32),
             V((nb, ch, blk), F32),
@@ -348,7 +381,8 @@
             V((line - 1, share, wide), BF16),
             V((line - 1, share, wide), BF16),
             V((n_grp, share, wide), BF16),
-            dma((6,)), dma((3,)),
+            V((8, links_wide), jnp.int32), pltpu.SMEM((8, links_wide), jnp.int32),
+            dma((7,)), dma((2,)),
             dma((n_dom, exports, 3)), dma((n_dom, exports)),
             dma((line,)), dma((line,)),
             dma((n_grp - 1, line)), dma((n_grp - 1, line)),
@@ -360,12 +394,23 @@
         ),
         cost_estimate=cost,
     )(
-        targets, counts, prev, last_of, wanted, features.reshape(nb, blk, ch), boundary_cache, adjacency,
+        neighbor.T, counts, wanted, features.reshape(nb, blk, ch), boundary_cache, adjacency,
         weight_in, weight_out, cotangent.reshape(tiles, TILE, ch),
     )
     scale = 1.0 / math.sqrt(node_rows * n_grp * n_dom)
-    gw_in, gw_out = (x.reshape(rows, -1).astype(F32) * scale for x in (gw_in, gw_out))
-    return out.reshape(node_rows, ch), gw_in, gw_out
+    out, gw_in, gw_out = pl.pallas_call(
+        functools.partial(finish_kernel, scale),
+        out_shape=(
+            jax.ShapeDtypeStruct((node_rows, ch), BF16),
+            jax.ShapeDtypeStruct((rows, hid_n), F32),
+            jax.ShapeDtypeStruct((rows, ch), F32),
+        ),
+        in_specs=[any_spec, vmem],
+        out_specs=(any_spec, vmem, vmem),
+        scratch_shapes=[dma((8 if node_rows % 128 == 0 else 1,))],
+        compiler_params=pltpu.CompilerParams(vmem_limit_bytes=56 * 2**20),
+    )(out.reshape(node_rows, ch), gw.reshape(rows, wide))
+    return out, gw_in, gw_out
 
 
 def local(

time: 49.2 us -> 90.2 us (1.83)
  Pallas kernels: 39.2 us -> 89.4 us
  other arithmetic: 6.42 us -> 0 us
  local copies, waits for them, and re-layouts: 2.65 us -> 0 us
    pallas_call x0 -> x1, Pallas kernels: none -> 50.4 us  [fast_local(): pl.pallas_call(functools.partial(finish_kernel, scale), out_shape=(jax.Sh...]
    mul x2 -> x0, other arithmetic: 2.9 us -> none  [fast_local(): x.reshape(rows, -1).astype(F32) * scale]
    reduce_max x2 -> x0, other arithmetic: 2.81 us -> none  [the longest x1 1.5 us: chains(): prev = jnp.max(jnp.where(same, place[None, None], 0), axis=(2, 3))]
    unnamed x1 -> x0, local copies, waits for them, and re-layouts: 2.65 us -> none
where the time goes in v1:
time: 90.2 us; the launch traced here: 90 us
  Pallas kernels  89.4 us (99%)
    pallas_call x1, Pallas kernels, fast_local(): pl.pallas_call(functools.partial(finish_kernel, scale), out_shape=(jax.Sh...  50.4 us
    pallas_call x1, Pallas kernels, fast_local(): pl.pallas_call(functools.partial(layer_kernel, n_grp, n_dom), out_shape=(...  39 us

profile of v1, /device:TPU:0, one launch (start us, length us, event | category | flops | bytes accessed | tf_op | source)
XLA Modules:
  0.0 90.0 jit_solution(1568550962506373109)
XLA Ops:
  0.6 39.0 %shard_map.112 = (bf16[24,128,256]{2,1,0:T(8,128)(2,1)}, bf16[4,16,768]{2,1,0:T(8,128)(2,1)}) custom-call(s32[2,24]{1,0:T(2,128)} %bitcast.9, s32[24]{0:T(128)} %cnt.1, s32[1,8]{1,0:T(1,128)} %wnt.1, bf16[24,128,256]{2,1,0:T(8,128)(2,1)} %bitcast.7, f32[256,256]{1,0:T(8,128)} %cache_h.1, bf16[24,2,128,128]{3,2,1,0:T(8,128)(2,1)} %adj_h.1, ...), custom_call_target="tpu_custom_call" | custom-call | flops 5637144576 | bytes 6291456 | tf_op jit(solution)/shard_map/pallas_call | solution.py:349
  39.7 50.4 %shard_map.113 = (bf16[3072,256]{1,0:T(8,128)(2,1)}, f32[64,512]{1,0:T(8,128)}, f32[64,256]{1,0:T(8,128)}) custom-call(bf16[3072,256]{1,0:T(8,128)(2,1)} %bitcast.5, bf16[64,768]{1,0:T(8,128)(2,1)} %bitcast.6), custom_call_target="tpu_custom_call" | custom-call | tf_op jit(solution)/shard_map/pallas_call | solution.py:401
